TPU v7x, 32 devices: a whole 2x2x4 slice. The times are simulated.
32 devices in a mesh: seq: 8 (over z, x), mp: 4 (over y, core).
Axes of the slice: x: 2, y: 2, z: 4, core: 2. Of those that a mesh axis runs over, the one named last changes fastest.
Arguments:
- win_query: bfloat16 [4096, 4096], P('seq', 'mp'), may hold values from -8 to 8
- win_key: bfloat16 [4096, 4096], P('seq', 'mp'), may hold values from -8 to 8
- win_value: bfloat16 [4096, 4096], P('seq', 'mp'), may hold values from -6 to 6
- win_dout: bfloat16 [4096, 4096], P('seq', 'mp'), may hold values from -16 to 16
- cross_query: bfloat16 [4096, 4096], P('seq', 'mp'), may hold values from -8 to 8
- cross_dout: bfloat16 [4096, 4096], P('seq', 'mp'), may hold values from -16 to 16
- patch_key: bfloat16 [1024, 4096], P('seq', 'mp'), may hold values from -8 to 8
- patch_value: bfloat16 [1024, 4096], P('seq', 'mp'), may hold values from -6 to 6
- patch_len: int32 [16, 64], P('seq'), may hold values from 1 to 16, 256 in all within a row
- patch_owner: int32 [1024, 1], P('seq'), may hold values from 0 to 7; in each aligned block of 128 rows (0 to 127, 128 to 255, ...) at most 32 rows name the same one
- w_query: bfloat16 [4096, 4096], P('seq', 'mp'), may hold values from -0.09375 to 0.09375
Outputs:
- win_dq: bfloat16 [4096, 4096], P('seq', 'mp')
- win_dk: bfloat16 [4096, 4096], P('seq', 'mp')
- win_dv: bfloat16 [4096, 4096], P('seq', 'mp')
- patch_grads: bfloat16 [2, 2048, 4096], P(None, 'seq', 'mp')
- byte_grads: bfloat16 [4096, 4096], P('seq', 'mp')
Inputs may be any that keep to these rules, and one draw needn't show every extreme that they name: `patch_len`: each row lists the byte lengths of the patches of one stored block in order; they sum to 256 and the largest is exactly 16. `patch_owner`: within each aligned block of 128 rows (the patch rows of one device) no owner is named more than 32 times, a bound that some block reaches.
All inputs are finite; a program needn't handle non-finite values.
Results may differ from a plain program's by a relative error of at most 0.017.
Values may be sent and summed in bfloat16 or wider, within the bound.
A program may use at most 128 MiB of HBM per device.

v0:
```python
import functools
import math

import jax
import jax.numpy as jnp
from jax import lax
from jax.experimental import pallas as pl
from jax.experimental.pallas import tpu as pltpu
from jax.sharding import PartitionSpec as P

HD = 128
WIN = 256
NT = (((1,), (1,)), ((), ()))
NN = (((1,), (0,)), ((), ()))
TN = (((0,), (0,)), ((), ()))


def dot(left, right, dims):
    return lax.dot_general(left, right, dims, preferred_element_type=jnp.float32)


def attention_grads(query, dout, keys, values, allowed):
    inv_root = 1.0 / math.sqrt(HD)
    scores = jnp.where(allowed, dot(query, keys, NT) * inv_root, -1e30)
    top = jnp.max(scores, axis=-1, keepdims=True)
    weights = jnp.where(allowed, jnp.exp(scores - top), 0.0)
    probs = weights * (1.0 / jnp.sum(weights, axis=-1, keepdims=True))
    dprobs = dot(dout, values, NT)
    delta = jnp.sum(probs * dprobs, axis=-1, keepdims=True)
    grad = (probs * (dprobs - delta) * inv_root).astype(jnp.bfloat16)
    return probs.astype(jnp.bfloat16), grad


def window_kernel(
    seq_count, q_ref, k_ref, v_ref, do_ref, before_ref, after_ref,
    dq_ref, dk_ref, dv_ref, low_ref, high_ref,
):
    seq_index = lax.axis_index("seq")
    is_last = seq_index == seq_count - 1
    rows_at = lax.broadcasted_iota(jnp.int32, (WIN, 2 * WIN), 0)
    cols_at = lax.broadcasted_iota(jnp.int32, (WIN, 2 * WIN), 1)
    gap = cols_at - rows_at
    inside = (gap >= 0) & (gap <= WIN)
    first_col = jnp.where(seq_index > 0, 0, WIN)
    low, high = slice(0, WIN), slice(WIN, 2 * WIN)

    def part(rows, rim_key, rim_value, allowed):
        query, dout = q_ref[rows, :], do_ref[rows, :]
        keys = jnp.concatenate([rim_key, k_ref[rows, :]], axis=0)
        values = jnp.concatenate([rim_value, v_ref[rows, :]], axis=0)
        probs, grad = attention_grads(query, dout, keys, values, allowed)
        dq_ref[rows, :] = dot(grad, keys, NN).astype(jnp.bfloat16)
        return dot(grad, query, TN), dot(probs, dout, TN)

    low_dk, low_dv = part(low, before_ref[0], before_ref[1], inside & (cols_at >= first_col))
    high_dk, high_dv = part(
        high,
        jnp.where(is_last, k_ref[low, :], after_ref[0]),
        jnp.where(is_last, v_ref[low, :], after_ref[1]),
        inside,
    )
    low_ref[0] = low_dk[:WIN].astype(jnp.bfloat16)
    low_ref[1] = low_dv[:WIN].astype(jnp.bfloat16)
    high_ref[0] = high_dk[:WIN].astype(jnp.bfloat16)
    high_ref[1] = high_dv[:WIN].astype(jnp.bfloat16)
    dk_ref[low, :] = (low_dk[WIN:] + jnp.where(is_last, high_dk[:WIN], 0.0)).astype(jnp.bfloat16)
    dv_ref[low, :] = (low_dv[WIN:] + jnp.where(is_last, high_dv[:WIN], 0.0)).astype(jnp.bfloat16)
    dk_ref[high, :] = high_dk[WIN:].astype(jnp.bfloat16)
    dv_ref[high, :] = high_dv[WIN:].astype(jnp.bfloat16)


def window_call(seq_count, query, key, value, dout, before, after):
    rows, width = query.shape
    heads = width // HD
    own = pl.BlockSpec((rows, HD), lambda h: (0, h))
    rim = pl.BlockSpec((2, WIN, HD), lambda h: (0, 0, h))
    full = jax.ShapeDtypeStruct((rows, width), jnp.bfloat16)
    rims = jax.ShapeDtypeStruct((2, WIN, width), jnp.bfloat16)
    return pl.pallas_call(
        functools.partial(window_kernel, seq_count),
        grid=(heads,),
        in_specs=[own, own, own, own, rim, rim],
        out_specs=[own, own, own, rim, rim],
        out_shape=[full, full, full, rims, rims],
        compiler_params=pltpu.CompilerParams(vmem_limit_bytes=60 << 20),
        cost_estimate=pl.CostEstimate(
            flops=heads * 10 * rows * 2 * WIN * HD,
            bytes_accessed=60 * rows * width,
            transcendentals=heads * rows * 2 * WIN,
        ),
        name="window",
    )(query, key, value, dout, before, after)


def join_kernel(dk_ref, dv_ref, low_ref, high_ref, out_dk_ref, out_dv_ref):
    for index, (own, out) in enumerate(((dk_ref, out_dk_ref), (dv_ref, out_dv_ref))):
        for part, back in enumerate((low_ref, high_ref)):
            rows = slice(part * WIN, (part + 1) * WIN)
            total = own[rows, :].astype(jnp.float32) + back[index].astype(jnp.float32)
            out[rows, :] = total.astype(jnp.bfloat16)


def join_call(own_dk, own_dv, low_back, high_back):
    rows, width = own_dk.shape
    tile = 2 * HD
    own = pl.BlockSpec((rows, tile), lambda h: (0, h))
    rim = pl.BlockSpec((2, WIN, tile), lambda h: (0, 0, h))
    full = jax.ShapeDtypeStruct((rows, width), jnp.bfloat16)
    return pl.pallas_call(
        join_kernel,
        grid=(width // tile,),
        in_specs=[own, own, rim, rim],
        out_specs=[own, own],
        out_shape=[full, full],
        compiler_params=pltpu.CompilerParams(vmem_limit_bytes=60 << 20),
        cost_estimate=pl.CostEstimate(
            flops=2 * rows * width, bytes_accessed=12 * rows * width, transcendentals=0
        ),
        name="join",
    )(own_dk, own_dv, low_back, high_back)


def cross_kernel(
    cap, q_ref, do_ref, k_ref, v_ref, len_ref, owner_col_ref, owner_row_ref, dq_ref, slots_ref
):
    rows, patches = q_ref.shape[0], k_ref.shape[0]
    block_rows, per_block = rows // 2, patches // 2
    earlier_at = lax.broadcasted_iota(jnp.int32, (patches, patches), 0)
    later_at = lax.broadcasted_iota(jnp.int32, (patches, patches), 1)
    before = earlier_at < later_at
    same_block = (earlier_at >= per_block) == (later_at >= per_block)
    starts = jnp.sum(jnp.where(before & same_block, len_ref[...], 0), axis=0, keepdims=True)
    same_owner = owner_col_ref[...] == owner_row_ref[...]
    rank = jnp.sum(jnp.where(before & same_owner, 1, 0), axis=0, keepdims=True)
    slot = owner_row_ref[...] * cap + rank
    rows_at = lax.broadcasted_iota(jnp.int32, (rows, patches), 0)
    cols_at = lax.broadcasted_iota(jnp.int32, (rows, patches), 1)
    upper_row, upper_col = rows_at >= block_rows, cols_at >= per_block
    within = jnp.where(upper_row, rows_at - block_rows, rows_at)
    allowed = (starts <= within) & (upper_row == upper_col)
    query, dout, keys, values = q_ref[...], do_ref[...], k_ref[...], v_ref[...]
    probs, grad = attention_grads(query, dout, keys, values, allowed)
    dq_ref[...] = dot(grad, keys, NN).astype(jnp.bfloat16)
    patch_dk = dot(grad, query, TN).astype(jnp.bfloat16)
    patch_dv = dot(probs, dout, TN).astype(jnp.bfloat16)
    slots = slots_ref.shape[1]
    chosen = lax.broadcasted_iota(jnp.int32, (slots, patches), 0) == slot
    selector = jnp.where(chosen, 1.0, 0.0).astype(jnp.bfloat16)
    slots_ref[0] = dot(selector, patch_dk, NN).astype(jnp.bfloat16)
    slots_ref[1] = dot(selector, patch_dv, NN).astype(jnp.bfloat16)


def cross_call(cap, slots, query, dout, key, value, lengths, owner):
    rows, width = query.shape
    patches = key.shape[0]
    heads = width // HD
    own = pl.BlockSpec((rows, HD), lambda h: (0, h))
    patch = pl.BlockSpec((patches, HD), lambda h: (0, h))
    column = pl.BlockSpec((patches, 1), lambda h: (0, 0))
    line = pl.BlockSpec((1, patches), lambda h: (0, 0))
    return pl.pallas_call(
        functools.partial(cross_kernel, cap),
        grid=(heads,),
        in_specs=[own, own, patch, patch, column, column, line],
        out_specs=[own, pl.BlockSpec((2, slots, HD), lambda h: (0, 0, h))],
        out_shape=[
            jax.ShapeDtypeStruct((rows, width), jnp.bfloat16),
            jax.ShapeDtypeStruct((2, slots, width), jnp.bfloat16),
        ],
        compiler_params=pltpu.CompilerParams(vmem_limit_bytes=60 << 20),
        cost_estimate=pl.CostEstimate(
            flops=heads * 12 * rows * patches * HD,
            bytes_accessed=8 * rows * width,
            transcendentals=heads * rows * patches,
        ),
        name="cross",
    )(query, dout, key, value, lengths.reshape(patches, 1), owner, owner.reshape(1, patches))


def target(place, me, count):
    if count != 4:
        return place
    row, core = me // 2, me % 2
    return (row if place % 2 else 1 - row) * 2 + (1 - core if place < 2 else core)


def parts_kernel(count, per_plane, *refs):
    dq_ref, w_refs = refs[0], refs[1 : 2 * count]
    send_ref, keep_ref, held, sems = refs[2 * count :]
    step = pl.program_id(0)
    plane = lax.axis_index("seq") // per_plane
    me = lax.axis_index("mp")

    @pl.when(step == 0)
    def _():
        for place in range(count):
            gap = target(place, me, count) - plane
            for index, w_ref in enumerate(w_refs):

                @pl.when(gap == index - (count - 1))
                def _(w_ref=w_ref, place=place):
                    pltpu.make_async_copy(w_ref, held.at[place], sems.at[place]).start()

    pltpu.make_async_copy(w_refs[0], held.at[step], sems.at[step]).wait()
    product = dot(dq_ref[...], held[step], NT).astype(jnp.bfloat16)

    @pl.when(step < count // 2)
    def _():
        send_ref[0] = product

    @pl.when(step >= count // 2)
    def _():
        keep_ref[0] = product


def parts_call(count, per_plane, dq, blocks):
    rows, width = dq.shape
    depth = blocks[0].shape[0]
    half = count // 2
    shape = jax.ShapeDtypeStruct((half, rows, depth), jnp.bfloat16)
    return pl.pallas_call(
        functools.partial(parts_kernel, count, per_plane),
        grid=(count,),
        in_specs=[pl.BlockSpec((rows, width), lambda j: (0, 0))]
        + [pl.BlockSpec(memory_space=pl.ANY)] * len(blocks),
        out_specs=[
            pl.BlockSpec((1, rows, depth), lambda j: (jnp.minimum(j, half - 1), 0, 0)),
            pl.BlockSpec((1, rows, depth), lambda j: (jnp.maximum(j - half, 0), 0, 0)),
        ],
        out_shape=[shape, shape],
        scratch_shapes=[
            pltpu.VMEM((count, depth, width), jnp.bfloat16),
            pltpu.SemaphoreType.DMA((count,)),
        ],
        compiler_params=pltpu.CompilerParams(vmem_limit_bytes=32 << 20),
        cost_estimate=pl.CostEstimate(
            flops=rows * width * depth,
            bytes_accessed=2 * rows * width,
            transcendentals=0,
        ),
        name="parts",
    )(dq, *blocks)


def plane_routes(planes, per_plane, hop):
    seq_count = planes * per_plane
    up = [
        (s, s + per_plane) for s in range(seq_count - per_plane) if s // per_plane >= hop - 1
    ]
    return up, [(seq_count - 1 - a, seq_count - 1 - b) for a, b in up]


def plane_step(up, down, planes, per_plane, hop):
    up_route, down_route = plane_routes(planes, per_plane, hop)
    return lax.ppermute(up, "seq", up_route), lax.ppermute(down, "seq", down_route)


def shifted(block, distance, count):
    route = [(i - distance, i) for i in range(count) if 0 <= i - distance < count]
    return lax.ppermute(block, "seq", route)


def turned(block, distance, count, per_plane):
    route = [
        (s, s - s % per_plane + (s % per_plane + distance) % per_plane) for s in range(count)
    ]
    return lax.ppermute(block, "seq", route)


def summed(send, keep, count):
    if count != 4:
        parts = jnp.concatenate([send, keep], axis=0)
        return lax.psum_scatter(parts, "mp", scatter_dimension=0, tiled=True)[0]
    arrived = lax.ppermute(send, "mp", [(m, m ^ 1) for m in range(count)])
    wide = arrived.astype(jnp.float32) + keep.astype(jnp.float32)
    across = lax.ppermute(wide[0].astype(jnp.bfloat16), "mp", [(m, m ^ 2) for m in range(count)])
    return (wide[1] + across.astype(jnp.float32)).astype(jnp.bfloat16)


def local(
    win_query,
    win_key,
    win_value,
    win_dout,
    cross_query,
    cross_dout,
    patch_key,
    patch_value,
    patch_len,
    patch_owner,
    w_query,
):
    seq_count, mp_count = lax.axis_size("seq"), lax.axis_size("mp")
    per_plane = seq_count // mp_count
    planes = mp_count
    column = lax.axis_index("seq") % per_plane
    width = win_query.shape[1]
    patch_rows = patch_key.shape[0]

    low_rim = jnp.stack([win_key[:WIN], win_value[:WIN]])
    high_rim = jnp.stack([win_key[WIN:], win_value[WIN:]])
    patch_len, low_rim, high_rim = lax.optimization_barrier((patch_len, low_rim, high_rim))
    before = shifted(low_rim, 1, seq_count)
    after = shifted(high_rim, -1, seq_count)
    up, down = {0: w_query}, {0: w_query}
    up[1], down[1] = plane_step(w_query, w_query, planes, per_plane, 1)
    cap = max(2, 2 * (patch_rows // seq_count))
    cross_dq, slots = cross_call(
        cap, seq_count * cap, cross_query, cross_dout, patch_key, patch_value, patch_len, patch_owner
    )
    all_dq = [cross_dq] + [
        turned(cross_dq, r, seq_count, per_plane) for r in range(1, per_plane)
    ]
    up[1], down[1], slots, before, after = lax.optimization_barrier(
        (up[1], down[1], slots, before, after)
    )
    up[2], down[2] = plane_step(up[1], down[1], planes, per_plane, 2)
    win_dq, own_dk, own_dv, low_send, high_send = window_call(
        seq_count, win_query, win_key, win_value, win_dout, before, after
    )
    low_back = shifted(low_send, -1, seq_count)
    high_back = shifted(high_send, 1, seq_count)
    up[2], down[2], win_dq, *all_dq = lax.optimization_barrier(
        (up[2], down[2], win_dq, *all_dq)
    )
    for hop in range(3, planes):
        up[hop], down[hop] = plane_step(up[hop - 1], down[hop - 1], planes, per_plane, hop)
    slots, win_dq = lax.optimization_barrier((slots, win_dq))
    arrived = lax.all_to_all(
        slots.reshape(2, seq_count, cap, width), "seq", split_axis=1, concat_axis=1, tiled=True
    )
    patch_grads = arrived.reshape(2, seq_count * cap, width)
    last = planes - 1
    up[last], down[last], patch_grads = lax.optimization_barrier(
        (up[last], down[last], patch_grads)
    )
    blocks = [up[hop] for hop in range(last, 0, -1)] + [down[hop] for hop in range(planes)]

    near = [None] * per_plane
    for r in range(per_plane - 1, -1, -1):
        if r == 0:
            all_dq[0], low_back, high_back = lax.optimization_barrier(
                (all_dq[0], low_back, high_back)
            )
        send, keep = parts_call(planes, per_plane, all_dq[r], blocks)
        total = summed(send, keep, mp_count)
        near[r] = turned(total, -r, seq_count, per_plane) if r else total
    win_dk, win_dv = join_call(own_dk, own_dv, low_back, high_back)
    pieces = []
    for j in range(per_plane):
        piece = near[j]
        for x in range(1, per_plane):
            piece = jnp.where(column == x, near[(j - x) % per_plane], piece)
        pieces.append(piece)
    byte_grads = jnp.concatenate(pieces, axis=1)
    return (win_dq, win_dk, win_dv, patch_grads, byte_grads)


def solution(mesh):
    in_specs = (P("seq", "mp"),) * 8 + (P("seq", None),) * 2 + (P("seq", "mp"),)
    out_specs = (P("seq", "mp"),) * 3 + (P(None, "seq", "mp"), P("seq", "mp"))
    return jax.shard_map(local, mesh=mesh, in_specs=in_specs, out_specs=out_specs, check_vma=False)
```

profile of v0, /device:TPU:0, one launch (start us, length us, event | category | flops | bytes accessed | tf_op | source)
XLA Modules:
  0.0 194.2 jit_solution(1725858847951392249)
XLA Ops:
  0.6 0.0 copy-start.4
  0.6 5.1 %collective-permute-start = (bf16[512,1024]{1,0:T(8,128)(2,1)}, bf16[512,1024]{1,0:T(8,128)(2,1)S(1)}, u32[]{:S(2)}, u32[]{:S(2)}) collective-permute-start(bf16[512,1024]{1,0:T(8,128)(2,1)} %refs_4_.3), channel_id=1, source_target_pairs={{0,8},{4,12},{8,16},{12,20},{16,24},{20,28},{1,9},{5,13},{9,17},{1... | collective-permute-start | bytes 3145736 | tf_op jit(solution)/shard_map/ppermute | solution.py:255
  5.8 1.3 collective-permute-start.1
  7.1 1.3 slice_bitcast_fusion.2
  8.4 0.1 slice_bitcast_fusion.3
  8.4 0.0 copy-start.5
  8.5 0.0 copy-start.6
  8.5 1.2 pad_maximum_fusion
  9.6 4.4 %collective-permute-start.2 = (bf16[2,256,1024]{2,1,0:T(8,128)(2,1)}, bf16[2,256,1024]{2,1,0:T(8,128)(2,1)}, u32[]{:S(2)}, u32[]{:S(2)}) collective-permute-start(bf16[2,256,1024]{2,1,0:T(8,128)(2,1)} %get-tuple-element.41), channel_id=1, source_target_pairs={{0,4},{4,8},{8,12},{12,16},{16,20},{20,24},{24,28},{1,5},{5,9},{9,... | collective-permute-start | bytes 3145736 | tf_op jit(solution)/shard_map/ppermute | solution.py:260
  14.0 1.3 collective-permute-start.3
  15.3 0.8 reshape.28.len_ref
  16.1 0.7 copy.22.owner_col_ref
  16.9 9.3 %cross.1 = (bf16[512,1024]{1,0:T(8,128)(2,1)}, bf16[2,256,1024]{2,1,0:T(8,128)(2,1)}) custom-call(bf16[512,1024]{1,0:T(8,128)(2,1)} %q_ref.2, bf16[512,1024]{1,0:T(8,128)(2,1)} %do_ref.2, bf16[128,1024]{1,0:T(8,128)(2,1)} %k_ref.2, bf16[128,1024]{1,0:T(8,128)(2,1)} %v_ref.2, s32[128,1]{1,0:T(8,128)} %reshape.28.len_ref, s32[128,1]{1,0:T(8,128)} %copy.22.owner_col_ref, ...), custom_call_target="tpu_custom_call" | custom-call | flops 805306368 | bytes 4194304 | tf_op jit(solution)/shard_map/cross/pallas_call | solution.py:161
  26.1 2.6 %collective-permute-start.6 = (bf16[512,1024]{1,0:T(8,128)(2,1)}, bf16[512,1024]{1,0:T(8,128)(2,1)}, u32[]{:S(2)}, u32[]{:S(2)}) collective-permute-start(bf16[512,1024]{1,0:T(8,128)(2,1)} %get-tuple-element.70.refs_0_), channel_id=1, source_target_pairs={{0,4},{4,0},{8,12},{12,8},{16,20},{20,16},{24,28},{28,24},{1,5},{5... | collective-permute-start | bytes 3145736 | tf_op jit(solution)/shard_map/ppermute | solution.py:267
  28.8 5.2 %collective-permute-done.1.refs_5_ = bf16[512,1024]{1,0:T(8,128)(2,1)S(1)} collective-permute-done((bf16[512,1024]{1,0:T(8,128)(2,1)}, bf16[512,1024]{1,0:T(8,128)(2,1)S(1)}, u32[]{:S(2)}, u32[]{:S(2)}) %collective-permute-start.1) | collective-permute-done | bytes 1048608 | tf_op jit(solution)/shard_map/ppermute | solution.py:255
  34.0 25.4 %collective-permute-done.2.before_ref = bf16[2,256,1024]{2,1,0:T(8,128)(2,1)} collective-permute-done((bf16[2,256,1024]{2,1,0:T(8,128)(2,1)}, bf16[2,256,1024]{2,1,0:T(8,128)(2,1)}, u32[]{:S(2)}, u32[]{:S(2)}) %collective-permute-start.2) | collective-permute-done | bytes 1048608 | tf_op jit(solution)/shard_map/ppermute | solution.py:260
  59.4 0.7 collective-permute-start.4
  60.1 1.3 collective-permute-start.5
  61.4 14.6 %window.1 = (bf16[512,1024]{1,0:T(8,128)(2,1)}, bf16[512,1024]{1,0:T(8,128)(2,1)}, bf16[512,1024]{1,0:T(8,128)(2,1)}, bf16[2,256,1024]{2,1,0:T(8,128)(2,1)}, bf16[2,256,1024]{2,1,0:T(8,128)(2,1)}) custom-call(bf16[512,1024]{1,0:T(8,128)(2,1)} %q_ref.3, bf16[512,1024]{1,0:T(8,128)(2,1)} %k_ref.3, bf16[512,1024]{1,0:T(8,128)(2,1)} %v_ref.3, ...), custom_call_target="tpu_custom_call" | custom-call | flops 2684354560 | bytes 31457280 | tf_op jit(solution)/shard_map/window/pallas_call | solution.py:79
  76.0 4.4 %collective-permute-done.6.refs_0_ = bf16[512,1024]{1,0:T(8,128)(2,1)} collective-permute-done((bf16[512,1024]{1,0:T(8,128)(2,1)}, bf16[512,1024]{1,0:T(8,128)(2,1)}, u32[]{:S(2)}, u32[]{:S(2)}) %collective-permute-start.6) | collective-permute-done | bytes 1048608 | tf_op jit(solution)/shard_map/ppermute | solution.py:267
  80.4 10.4 %collective-permute-done.5.refs_6_ = bf16[512,1024]{1,0:T(8,128)(2,1)} collective-permute-done((bf16[512,1024]{1,0:T(8,128)(2,1)S(1)}, bf16[512,1024]{1,0:T(8,128)(2,1)}, u32[]{:S(2)}, u32[]{:S(2)}) %collective-permute-start.5) | collective-permute-done | bytes 1048608 | tf_op jit(solution)/shard_map/ppermute | solution.py:255
  90.8 2.3 %copy.23 = bf16[2,8,32,1024]{3,2,0,1:T(8,128)(2,1)} copy(bf16[2,8,32,1024]{3,2,1,0:T(8,128)(2,1)} %bitcast.32) | data formatting | bytes 2097152 | tf_op jit(solution)/shard_map/reshape | solution.py:330
  93.1 4.4 %all-to-all-start = ((bf16[2,8,32,1024]{3,2,0,1:T(8,128)(2,1)}), bf16[2,8,32,1024]{3,2,0,1:T(8,128)(2,1)}, u32[]{:S(2)}, u32[]{:S(2)}) async-start(bf16[2,8,32,1024]{3,2,0,1:T(8,128)(2,1)} %copy.23), calls=%async_computation | async-start | bytes 2097152 | tf_op jit(solution)/shard_map/all_to_all | solution.py:329
  97.5 1.6 collective-permute-start.9
  99.1 1.3 collective-permute-start.10
  100.4 1.3 collective-permute-start.7
  101.7 5.6 %collective-permute-start.8 = (bf16[2,256,1024]{2,1,0:T(8,128)(2,1)}, bf16[2,256,1024]{2,1,0:T(8,128)(2,1)}, u32[]{:S(2)}, u32[]{:S(2)}) collective-permute-start(bf16[2,256,1024]{2,1,0:T(8,128)(2,1)} %get-tuple-element.56), channel_id=1, source_target_pairs={{0,4},{4,8},{8,12},{12,16},{16,20},{20,24},{24,28},{1,5},{5,9},{9,... | collective-permute-start | bytes 3145736 | tf_op jit(solution)/shard_map/ppermute | solution.py:260
  107.2 15.6 %all-to-all-done = bf16[2,8,32,1024]{3,2,0,1:T(8,128)(2,1)} async-done(((bf16[2,8,32,1024]{3,2,0,1:T(8,128)(2,1)}), bf16[2,8,32,1024]{3,2,0,1:T(8,128)(2,1)}, u32[]{:S(2)}, u32[]{:S(2)}) %all-to-all-start) | async-done | bytes 1048608 | tf_op jit(solution)/shard_map/all_to_all | solution.py:329
  122.8 2.4 %copy.24 = bf16[2,8,32,1024]{3,2,1,0:T(8,128)(2,1)} copy(bf16[2,8,32,1024]{3,2,0,1:T(8,128)(2,1)} %all-to-all-done) | data formatting | bytes 2097152 | tf_op jit(solution)/shard_map/all_to_all | solution.py:329
  125.2 13.5 %collective-permute-done.10.refs_7_ = bf16[512,1024]{1,0:T(8,128)(2,1)} collective-permute-done((bf16[512,1024]{1,0:T(8,128)(2,1)}, bf16[512,1024]{1,0:T(8,128)(2,1)}, u32[]{:S(2)}, u32[]{:S(2)}) %collective-permute-start.10) | collective-permute-done | bytes 1048608 | tf_op jit(solution)/shard_map/ppermute | solution.py:255
  138.8 5.8 %parts.2 = (bf16[2,512,512]{2,1,0:T(8,128)(2,1)S(1)}, bf16[2,512,512]{2,1,0:T(8,128)(2,1)S(1)}) custom-call(bf16[512,1024]{1,0:T(8,128)(2,1)} %collective-permute-done.6.refs_0_, bf16[512,1024]{1,0:T(8,128)(2,1)} %collective-permute-done.9.refs_1_, bf16[512,1024]{1,0:T(8,128)(2,1)S(1)} %copy-done.2, bf16[512,1024]{1,0:T(8,128)(2,1)S(1)} %collective-permute-done.refs_3_, ...), custom_call_target="tpu_custom_call" | custom-call | flops 268435456 | bytes 1048576 | tf_op jit(solution)/shard_map/parts/pallas_call | solution.py:221
  144.6 0.1 collective-permute-start.11
  144.7 4.6 %parts.3 = (bf16[2,512,512]{2,1,0:T(8,128)(2,1)S(1)}, bf16[2,512,512]{2,1,0:T(8,128)(2,1)S(1)}) custom-call(bf16[512,1024]{1,0:T(8,128)(2,1)S(1)} %copy-done.3, bf16[512,1024]{1,0:T(8,128)(2,1)} %collective-permute-done.9.refs_1_, bf16[512,1024]{1,0:T(8,128)(2,1)S(1)} %copy-done.2, bf16[512,1024]{1,0:T(8,128)(2,1)S(1)} %collective-permute-done.refs_3_, ...), custom_call_target="tpu_custom_call" | custom-call | flops 268435456 | bytes 1048576 | tf_op jit(solution)/shard_map/parts/pallas_call | solution.py:221
  149.3 0.5 collective-permute-start.14
  149.8 0.3 convert_add_fusion.1
  150.2 0.1 fusion.4
  150.2 0.1 collective-permute-start.12
  150.4 1.7 collective-permute-done.14
  152.1 0.3 convert_add_fusion
  152.4 0.1 fusion.5
  152.5 0.3 collective-permute-start.15
  152.8 12.3 %collective-permute-done.12 = bf16[512,512]{1,0:T(8,128)(2,1)S(1)} collective-permute-done((bf16[512,512]{1,0:T(8,128)(2,1)S(1)}, bf16[512,512]{1,0:T(8,128)(2,1)S(1)}, u32[]{:S(2)}, u32[]{:S(2)}) %collective-permute-start.12) | collective-permute-done | bytes 524320 | tf_op jit(solution)/shard_map/ppermute | solution.py:276
  165.1 1.0 fusion.3
  166.1 14.0 %collective-permute-start.13 = (bf16[512,512]{1,0:T(8,128)(2,1)}, bf16[512,512]{1,0:T(8,128)(2,1)}, u32[]{:S(2)}, u32[]{:S(2)}) collective-permute-start(bf16[512,512]{1,0:T(8,128)(2,1)} %fusion.3), channel_id=1, source_target_pairs={{0,4},{4,0},{8,12},{12,8},{16,20},{20,16},{24,28},{28,24},{1,5},{5... | collective-permute-start | bytes 1572872 | tf_op jit(solution)/shard_map/ppermute | solution.py:267
  180.1 4.2 %join.1 = (bf16[512,1024]{1,0:T(8,128)(2,1)}, bf16[512,1024]{1,0:T(8,128)(2,1)}) custom-call(bf16[512,1024]{1,0:T(8,128)(2,1)} %get-tuple-element.52.dk_ref, bf16[512,1024]{1,0:T(8,128)(2,1)} %get-tuple-element.53.dv_ref, bf16[2,256,1024]{2,1,0:T(8,128)(2,1)} %collective-permute-done.7.low_ref, bf16[2,256,1024]{2,1,0:T(8,128)(2,1)} %collective-permute-done.8.high_ref), custom_call_target="tpu_custom_call" | custom-call | flops 1048576 | bytes 6291456 | tf_op jit(solution)/shard_map/join/pallas_call | solution.py:109
  184.3 7.5 %collective-permute-done.13 = bf16[512,512]{1,0:T(8,128)(2,1)} collective-permute-done((bf16[512,512]{1,0:T(8,128)(2,1)}, bf16[512,512]{1,0:T(8,128)(2,1)}, u32[]{:S(2)}, u32[]{:S(2)}) %collective-permute-start.13) | collective-permute-done | bytes 524320 | tf_op jit(solution)/shard_map/ppermute | solution.py:267
  191.8 1.3 broadcast_select_fusion.1
  193.1 1.1 pad_maximum_fusion.2
  (19 shorter events, 0.0 us)
Async XLA Ops:
  0.6 7.7 %copy-start.4 = (bf16[512,1024]{1,0:T(8,128)(2,1)S(1)}, bf16[512,1024]{1,0:T(8,128)(2,1)}, u32[]{:S(2)}) copy-start(bf16[512,1024]{1,0:T(8,128)(2,1)} %k_ref.3) | copy-start | bytes 3145732
  0.6 28.1 %collective-permute-start = (bf16[512,1024]{1,0:T(8,128)(2,1)}, bf16[512,1024]{1,0:T(8,128)(2,1)S(1)}, u32[]{:S(2)}, u32[]{:S(2)}) collective-permute-start(bf16[512,1024]{1,0:T(8,128)(2,1)} %refs_4_.3), channel_id=1, source_target_pairs={{0,8},{4,12},{8,16},{12,20},{16,24},{20,28},{1,9},{5,13},{9,17},{1... | collective-permute-start | bytes 3145736 | tf_op jit(solution)/shard_map/ppermute | solution.py:255
  5.8 28.2 %collective-permute-start.1 = (bf16[512,1024]{1,0:T(8,128)(2,1)}, bf16[512,1024]{1,0:T(8,128)(2,1)S(1)}, u32[]{:S(2)}, u32[]{:S(2)}) collective-permute-start(bf16[512,1024]{1,0:T(8,128)(2,1)} %refs_4_.3), channel_id=1, source_target_pairs={{28,20},{24,16},{20,12},{16,8},{12,4},{8,0},{29,21},{25,17},{21,13... | collective-permute-start | bytes 3145736 | tf_op jit(solution)/shard_map/ppermute | solution.py:255
  8.4 6.9 %copy-start.5 = (s32[2,64]{1,0:T(2,128)S(1)}, s32[2,64]{1,0:T(2,128)}, u32[]{:S(2)}) copy-start(s32[2,64]{1,0:T(2,128)} %param.19) | copy-start | bytes 1540
  8.5 7.7 %copy-start.6 = (s32[128,1]{0,1:T(1,128)S(1)}, s32[128,1]{0,1:T(1,128)}, u32[]{:S(2)}) copy-start(s32[128,1]{0,1:T(1,128)} %param.20) | copy-start | bytes 1540
  9.6 49.8 %collective-permute-start.2 = (bf16[2,256,1024]{2,1,0:T(8,128)(2,1)}, bf16[2,256,1024]{2,1,0:T(8,128)(2,1)}, u32[]{:S(2)}, u32[]{:S(2)}) collective-permute-start(bf16[2,256,1024]{2,1,0:T(8,128)(2,1)} %get-tuple-element.41), channel_id=1, source_target_pairs={{0,4},{4,8},{8,12},{12,16},{16,20},{20,24},{24,28},{1,5},{5,9},{9,... | collective-permute-start | bytes 3145736 | tf_op jit(solution)/shard_map/ppermute | solution.py:260
  14.0 45.3 %collective-permute-start.3 = (bf16[2,256,1024]{2,1,0:T(8,128)(2,1)S(1)}, bf16[2,256,1024]{2,1,0:T(8,128)(2,1)}, u32[]{:S(2)}, u32[]{:S(2)}) collective-permute-start(bf16[2,256,1024]{2,1,0:T(8,128)(2,1)S(1)} %get-tuple-element.42), channel_id=1, source_target_pairs={{4,0},{8,4},{12,8},{16,12},{20,16},{24,20},{28,24},{5,1},{9,5},{13... | collective-permute-start | bytes 3145736 | tf_op jit(solution)/shard_map/ppermute | solution.py:260
  26.1 54.2 %collective-permute-start.6 = (bf16[512,1024]{1,0:T(8,128)(2,1)}, bf16[512,1024]{1,0:T(8,128)(2,1)}, u32[]{:S(2)}, u32[]{:S(2)}) collective-permute-start(bf16[512,1024]{1,0:T(8,128)(2,1)} %get-tuple-element.70.refs_0_), channel_id=1, source_target_pairs={{0,4},{4,0},{8,12},{12,8},{16,20},{20,16},{24,28},{28,24},{1,5},{5... | collective-permute-start | bytes 3145736 | tf_op jit(solution)/shard_map/ppermute | solution.py:267
  59.4 21.0 %collective-permute-start.4 = (bf16[512,1024]{1,0:T(8,128)(2,1)S(1)}, bf16[512,1024]{1,0:T(8,128)(2,1)S(1)}, u32[]{:S(2)}, u32[]{:S(2)}) collective-permute-start(bf16[512,1024]{1,0:T(8,128)(2,1)S(1)} %collective-permute-done.refs_3_), channel_id=1, source_target_pairs={{8,16},{12,20},{16,24},{20,28},{9,17},{13,21},{17,25},{21,29},{10,... | collective-permute-start | bytes 3145736 | tf_op jit(solution)/shard_map/ppermute | solution.py:255
  60.1 30.7 %collective-permute-start.5 = (bf16[512,1024]{1,0:T(8,128)(2,1)S(1)}, bf16[512,1024]{1,0:T(8,128)(2,1)}, u32[]{:S(2)}, u32[]{:S(2)}) collective-permute-start(bf16[512,1024]{1,0:T(8,128)(2,1)S(1)} %collective-permute-done.1.refs_5_), channel_id=1, source_target_pairs={{20,12},{16,8},{12,4},{8,0},{21,13},{17,9},{13,5},{9,1},{22,14},{1... | collective-permute-start | bytes 3145736 | tf_op jit(solution)/shard_map/ppermute | solution.py:255
  80.4 10.4 %copy-start.1 = (bf16[512,1024]{1,0:T(8,128)(2,1)}, bf16[512,1024]{1,0:T(8,128)(2,1)S(1)}, u32[]{:S(2)}) copy-start(bf16[512,1024]{1,0:T(8,128)(2,1)S(1)} %collective-permute-done.4.refs_2_) | copy-start | bytes 3145732
  93.1 45.7 %copy-start = (bf16[512,1024]{1,0:T(8,128)(2,1)S(1)}, bf16[512,1024]{1,0:T(8,128)(2,1)}, u32[]{:S(2)}) copy-start(bf16[512,1024]{1,0:T(8,128)(2,1)} %refs_4_.3) | copy-start | bytes 3145732
  93.1 29.7 %all-to-all-start = ((bf16[2,8,32,1024]{3,2,0,1:T(8,128)(2,1)}), bf16[2,8,32,1024]{3,2,0,1:T(8,128)(2,1)}, u32[]{:S(2)}, u32[]{:S(2)}) async-start(bf16[2,8,32,1024]{3,2,0,1:T(8,128)(2,1)} %copy.23), calls=%async_computation | async-start | bytes 2097152 | tf_op jit(solution)/shard_map/all_to_all | solution.py:329
  97.5 27.7 %collective-permute-start.9 = (bf16[512,1024]{1,0:T(8,128)(2,1)}, bf16[512,1024]{1,0:T(8,128)(2,1)}, u32[]{:S(2)}, u32[]{:S(2)}) collective-permute-start(bf16[512,1024]{1,0:T(8,128)(2,1)} %copy-done.1), channel_id=1, source_target_pairs={{16,24},{20,28},{17,25},{21,29},{18,26},{22,30},{19,27},{23,31}} | collective-permute-start | bytes 3145736 | tf_op jit(solution)/shard_map/ppermute | solution.py:255
  99.1 39.6 %collective-permute-start.10 = (bf16[512,1024]{1,0:T(8,128)(2,1)}, bf16[512,1024]{1,0:T(8,128)(2,1)}, u32[]{:S(2)}, u32[]{:S(2)}) collective-permute-start(bf16[512,1024]{1,0:T(8,128)(2,1)} %collective-permute-done.5.refs_6_), channel_id=1, source_target_pairs={{12,4},{8,0},{13,5},{9,1},{14,6},{10,2},{15,7},{11,3}} | collective-permute-start | bytes 3145736 | tf_op jit(solution)/shard_map/ppermute | solution.py:255
  100.4 44.3 %collective-permute-start.7 = (bf16[2,256,1024]{2,1,0:T(8,128)(2,1)}, bf16[2,256,1024]{2,1,0:T(8,128)(2,1)}, u32[]{:S(2)}, u32[]{:S(2)}) collective-permute-start(bf16[2,256,1024]{2,1,0:T(8,128)(2,1)} %get-tuple-element.55), channel_id=1, source_target_pairs={{4,0},{8,4},{12,8},{16,12},{20,16},{24,20},{28,24},{5,1},{9,5},{13... | collective-permute-start | bytes 3145736 | tf_op jit(solution)/shard_map/ppermute | solution.py:260
  101.7 43.0 %collective-permute-start.8 = (bf16[2,256,1024]{2,1,0:T(8,128)(2,1)}, bf16[2,256,1024]{2,1,0:T(8,128)(2,1)}, u32[]{:S(2)}, u32[]{:S(2)}) collective-permute-start(bf16[2,256,1024]{2,1,0:T(8,128)(2,1)} %get-tuple-element.56), channel_id=1, source_target_pairs={{0,4},{4,8},{8,12},{12,16},{16,20},{20,24},{24,28},{1,5},{5,9},{9,... | collective-permute-start | bytes 3145736 | tf_op jit(solution)/shard_map/ppermute | solution.py:260
  122.8 15.9 %copy-start.2 = (bf16[512,1024]{1,0:T(8,128)(2,1)S(1)}, bf16[512,1024]{1,0:T(8,128)(2,1)}, u32[]{:S(2)}) copy-start(bf16[512,1024]{1,0:T(8,128)(2,1)} %copy-done.1) | copy-start | bytes 3145732
  138.8 5.9 %copy-start.3 = (bf16[512,1024]{1,0:T(8,128)(2,1)S(1)}, bf16[512,1024]{1,0:T(8,128)(2,1)}, u32[]{:S(2)}) copy-start(bf16[512,1024]{1,0:T(8,128)(2,1)} %get-tuple-element.70.refs_0_) | copy-start | bytes 3145732
  144.6 5.2 %collective-permute-start.11 = (bf16[2,512,512]{2,1,0:T(8,128)(2,1)S(1)}, bf16[2,512,512]{2,1,0:T(8,128)(2,1)S(1)}, u32[]{:S(2)}, u32[]{:S(2)}) collective-permute-start(bf16[2,512,512]{2,1,0:T(8,128)(2,1)S(1)} %get-tuple-element.68), channel_id=1, source_target_pairs={{0,1},{1,0},{2,3},{3,2},{4,5},{5,4},{6,7},{7,6},{8,9},{9,8},{10,11... | collective-permute-start | bytes 3145736 | tf_op jit(solution)/shard_map/ppermute | solution.py:274
  149.3 2.8 %collective-permute-start.14 = (bf16[2,512,512]{2,1,0:T(8,128)(2,1)S(1)}, bf16[2,512,512]{2,1,0:T(8,128)(2,1)S(1)}, u32[]{:S(2)}, u32[]{:S(2)}) collective-permute-start(bf16[2,512,512]{2,1,0:T(8,128)(2,1)S(1)} %get-tuple-element.71), channel_id=1, source_target_pairs={{0,1},{1,0},{2,3},{3,2},{4,5},{5,4},{6,7},{7,6},{8,9},{9,8},{10,11... | collective-permute-start | bytes 3145736 | tf_op jit(solution)/shard_map/ppermute | solution.py:274
  150.2 14.8 %collective-permute-start.12 = (bf16[512,512]{1,0:T(8,128)(2,1)S(1)}, bf16[512,512]{1,0:T(8,128)(2,1)S(1)}, u32[]{:S(2)}, u32[]{:S(2)}) collective-permute-start(bf16[512,512]{1,0:T(8,128)(2,1)S(1)} %fusion.4), channel_id=1, source_target_pairs={{0,2},{1,3},{2,0},{3,1},{4,6},{5,7},{6,4},{7,5},{8,10},{9,11},{10,... | collective-permute-start | bytes 1572872 | tf_op jit(solution)/shard_map/ppermute | solution.py:276
  152.5 31.8 %collective-permute-start.15 = (bf16[512,512]{1,0:T(8,128)(2,1)S(1)}, bf16[512,512]{1,0:T(8,128)(2,1)S(1)}, u32[]{:S(2)}, u32[]{:S(2)}) collective-permute-start(bf16[512,512]{1,0:T(8,128)(2,1)S(1)} %fusion.5), channel_id=1, source_target_pairs={{0,2},{1,3},{2,0},{3,1},{4,6},{5,7},{6,4},{7,5},{8,10},{9,11},{10,... | collective-permute-start | bytes 1572872 | tf_op jit(solution)/shard_map/ppermute | solution.py:276
  166.1 25.7 %collective-permute-start.13 = (bf16[512,512]{1,0:T(8,128)(2,1)}, bf16[512,512]{1,0:T(8,128)(2,1)}, u32[]{:S(2)}, u32[]{:S(2)}) collective-permute-start(bf16[512,512]{1,0:T(8,128)(2,1)} %fusion.3), channel_id=1, source_target_pairs={{0,4},{4,0},{8,12},{12,8},{16,20},{20,16},{24,28},{28,24},{1,5},{5... | collective-permute-start | bytes 1572872 | tf_op jit(solution)/shard_map/ppermute | solution.py:267
where the time goes:
time: 195 us; the launch traced here: 194 us
  waiting for transfers between devices  96.1 us (49%)
  starting transfers between devices  45.9 us (24%)
  Pallas kernels  38.4 us (20%)
  local copies, waits for them, and re-layouts  7.7 us (4%)
  other arithmetic  5.18 us (3%)
    ppermute x3, waiting for transfers between devices, plane_step(): lax.ppermute(down, 'seq', down_route)  29.1 us
    ppermute x4, waiting for transfers between devices, shifted(): return lax.ppermute(block, 'seq', route)  25.4 us
    ppermute x2, starting transfers between devices, turned(): return lax.ppermute(block, 'seq', route)  16.7 us
    all_to_all x1, waiting for transfers between devices, local(): lax.all_to_all(slots.reshape(2, seq_count, cap, width), 'seq', split_axis...  15.6 us
    pallas_call x1, Pallas kernels, window_call(): pl.pallas_call(functools.partial(window_kernel, seq_count), grid=(heads,)...  14.6 us
    ppermute x4, starting transfers between devices, shifted(): return lax.ppermute(block, 'seq', route)  12.5 us
    ppermute x2, waiting for transfers between devices, summed(): lax.ppermute(wide[0].astype(jnp.bfloat16), 'mp', [(m, m ^ 2) for m in ran...  12.3 us
    ppermute x2, waiting for transfers between devices, turned(): return lax.ppermute(block, 'seq', route)  11.9 us
  transfers between devices with their start and end apart: 17, of which 9 were waited for; matrix products, arithmetic and copies ran while one was open for 4% of the time, Pallas kernels for 20%

commit v1 on v0

--- a/solution.py
+++ b/solution.py
@@ -325,15 +325,7 @@
     )
     for hop in range(3, planes):
         up[hop], down[hop] = plane_step(up[hop - 1], down[hop - 1], planes, per_plane, hop)
-    slots, win_dq = lax.optimization_barrier((slots, win_dq))
-    arrived = lax.all_to_all(
-        slots.reshape(2, seq_count, cap, width), "seq", split_axis=1, concat_axis=1, tiled=True
-    )
-    patch_grads = arrived.reshape(2, seq_count * cap, width)
     last = planes - 1
-    up[last], down[last], patch_grads = lax.optimization_barrier(
-        (up[last], down[last], patch_grads)
-    )
     blocks = [up[hop] for hop in range(last, 0, -1)] + [down[hop] for hop in range(planes)]
 
     near = [None] * per_plane
@@ -343,6 +335,11 @@
                 (all_dq[0], low_back, high_back)
             )
         send, keep = parts_call(planes, per_plane, all_dq[r], blocks)
+        if r == per_plane - 1:
+            slots, send = lax.optimization_barrier((slots, send))
+            arrived = lax.all_to_all(
+                slots.reshape(2, seq_count, cap, width), "seq", split_axis=1, concat_axis=1, tiled=True
+            )
         total = summed(send, keep, mp_count)
         near[r] = turned(total, -r, seq_count, per_plane) if r else total
     win_dk, win_dv = join_call(own_dk, own_dv, low_back, high_back)
@@ -353,6 +350,7 @@
             piece = jnp.where(column == x, near[(j - x) % per_plane], piece)
         pieces.append(piece)
     byte_grads = jnp.concatenate(pieces, axis=1)
+    patch_grads = arrived.reshape(2, seq_count * cap, width)
     return (win_dq, win_dk, win_dv, patch_grads, byte_grads)
 
 

time: 195 us -> 187 us (0.959)
  starting transfers between devices: 45.9 us -> 34.3 us
  other arithmetic: 5.18 us -> 8.17 us
  local copies, waits for them, and re-layouts: 7.7 us -> 9.83 us
  waiting for transfers between devices: 96.1 us -> 94.1 us
    ppermute x4, waiting for transfers between devices: 25.4 us -> 38.3 us  [shifted(): return lax.ppermute(block, 'seq', route)]
    all_to_all x1, waiting for transfers between devices: 15.6 us -> 2.72 us  [local(): lax.all_to_all(slots.reshape(2, seq_count, cap, width), 'seq', split_axis...]
    ppermute x2, starting transfers between devices: 16.7 us -> 5.24 us  [turned(): return lax.ppermute(block, 'seq', route)]
    ppermute x3, waiting for transfers between devices: 29.1 us -> 37.7 us  [plane_step(): lax.ppermute(down, 'seq', down_route)]
    ppermute x2, waiting for transfers between devices: 11.9 us -> 6.06 us  [turned(): return lax.ppermute(block, 'seq', route)]
    unnamed x15 -> x29, local copies, waits for them, and re-layouts: 0.77 us -> 4.65 us
    ppermute x2, waiting for transfers between devices: 12.3 us -> 9.36 us  [summed(): lax.ppermute(wide[0].astype(jnp.bfloat16), 'mp', [(m, m ^ 2) for m in ran...]
    add x2, other arithmetic: 0.64 us -> 3.13 us  [summed(): wide = arrived.astype(jnp.float32) + keep.astype(jnp.float32)]
  transfers between devices with their start and end apart: 17 -> 17, of which waited for: 9 -> 9; matrix products, arithmetic and copies ran while one was open for 4% -> 6% of each run, Pallas kernels for 20% -> 21%
where the time goes in v1:
time: 187 us; the launch traced here: 186 us
  waiting for transfers between devices  94.1 us (50%)
  Pallas kernels  38.2 us (20%)
  starting transfers between devices  34.3 us (18%)
  local copies, waits for them, and re-layouts  9.83 us (5%)
  other arithmetic  8.17 us (4%)
    ppermute x4, waiting for transfers between devices, shifted(): return lax.ppermute(block, 'seq', route)  38.3 us
    ppermute x3, waiting for transfers between devices, plane_step(): lax.ppermute(down, 'seq', down_route)  37.7 us
    pallas_call x1, Pallas kernels, window_call(): pl.pallas_call(functools.partial(window_kernel, seq_count), grid=(heads,)...  14.6 us
    ppermute x4, starting transfers between devices, shifted(): return lax.ppermute(block, 'seq', route)  10.8 us
    pallas_call x2, Pallas kernels, parts_call(): pl.pallas_call(functools.partial(parts_kernel, count, per_plane), grid=(c...  10.1 us
    ppermute x2, waiting for transfers between devices, summed(): lax.ppermute(wide[0].astype(jnp.bfloat16), 'mp', [(m, m ^ 2) for m in ran...  9.36 us
    pallas_call x1, Pallas kernels, cross_call(): pl.pallas_call(functools.partial(cross_kernel, cap), grid=(heads,), in_sp...  9.35 us
    ppermute x3, starting transfers between devices, plane_step(): lax.ppermute(up, 'seq', up_route)  7.64 us
  transfers between devices with their start and end apart: 17, of which 9 were waited for; matrix products, arithmetic and copies ran while one was open for 6% of the time, Pallas kernels for 21%

profile of v1, /device:TPU:0, one launch (start us, length us, event | category | flops | bytes accessed | tf_op | source)
XLA Modules:
  0.0 185.5 jit_solution(4476201905746793979)
XLA Ops:
  0.6 5.1 %collective-permute-start = (bf16[512,1024]{1,0:T(8,128)(2,1)}, bf16[512,1024]{1,0:T(8,128)(2,1)S(1)}, u32[]{:S(2)}, u32[]{:S(2)}) collective-permute-start(bf16[512,1024]{1,0:T(8,128)(2,1)} %refs_4_.3), channel_id=1, source_target_pairs={{0,8},{4,12},{8,16},{12,20},{16,24},{20,28},{1,9},{5,13},{9,17},{1... | collective-permute-start | bytes 3145736 | tf_op jit(solution)/shard_map/ppermute | solution.py:255
  5.8 1.3 collective-permute-start.1
  7.1 1.3 slice_bitcast_fusion.2
  8.4 0.1 slice_bitcast_fusion.3
  8.5 1.5 pad_maximum_fusion
  10.0 3.4 %collective-permute-start.2 = (bf16[2,256,1024]{2,1,0:T(8,128)(2,1)}, bf16[2,256,1024]{2,1,0:T(8,128)(2,1)S(1)}, u32[]{:S(2)}, u32[]{:S(2)}) collective-permute-start(bf16[2,256,1024]{2,1,0:T(8,128)(2,1)} %get-tuple-element.38), channel_id=1, source_target_pairs={{0,4},{4,8},{8,12},{12,16},{16,20},{20,24},{24,28},{1,5},{5,9},{9,... | collective-permute-start | bytes 3145736 | tf_op jit(solution)/shard_map/ppermute | solution.py:260
  13.4 1.3 collective-permute-start.3
  14.7 0.8 reshape.28.len_ref
  15.5 0.7 copy.22.owner_col_ref
  16.2 9.3 %cross.1 = (bf16[512,1024]{1,0:T(8,128)(2,1)}, bf16[2,256,1024]{2,1,0:T(8,128)(2,1)}) custom-call(bf16[512,1024]{1,0:T(8,128)(2,1)} %q_ref.2, bf16[512,1024]{1,0:T(8,128)(2,1)} %do_ref.2, bf16[128,1024]{1,0:T(8,128)(2,1)} %k_ref.2, bf16[128,1024]{1,0:T(8,128)(2,1)} %v_ref.2, s32[128,1]{1,0:T(8,128)} %reshape.28.len_ref, s32[128,1]{1,0:T(8,128)} %copy.22.owner_col_ref, ...), custom_call_target="tpu_custom_call" | custom-call | flops 805306368 | bytes 4194304 | tf_op jit(solution)/shard_map/cross/pallas_call | solution.py:161
  25.6 3.2 %collective-permute-start.6 = (bf16[512,1024]{1,0:T(8,128)(2,1)}, bf16[512,1024]{1,0:T(8,128)(2,1)}, u32[]{:S(2)}, u32[]{:S(2)}) collective-permute-start(bf16[512,1024]{1,0:T(8,128)(2,1)} %get-tuple-element.64.refs_0_), channel_id=1, source_target_pairs={{0,4},{4,0},{8,12},{12,8},{16,20},{20,16},{24,28},{28,24},{1,5},{5... | collective-permute-start | bytes 3145736 | tf_op jit(solution)/shard_map/ppermute | solution.py:267
  28.8 5.2 %collective-permute-done.1.refs_5_ = bf16[512,1024]{1,0:T(8,128)(2,1)S(1)} collective-permute-done((bf16[512,1024]{1,0:T(8,128)(2,1)}, bf16[512,1024]{1,0:T(8,128)(2,1)S(1)}, u32[]{:S(2)}, u32[]{:S(2)}) %collective-permute-start.1) | collective-permute-done | bytes 1048608 | tf_op jit(solution)/shard_map/ppermute | solution.py:255
  34.0 25.8 %collective-permute-done.2.before_ref = bf16[2,256,1024]{2,1,0:T(8,128)(2,1)S(1)} collective-permute-done((bf16[2,256,1024]{2,1,0:T(8,128)(2,1)}, bf16[2,256,1024]{2,1,0:T(8,128)(2,1)S(1)}, u32[]{:S(2)}, u32[]{:S(2)}) %collective-permute-start.2) | collective-permute-done | bytes 1048608 | tf_op jit(solution)/shard_map/ppermute | solution.py:260
  59.7 1.0 copy-done.13
  60.7 1.8 collective-permute-start.4
  62.5 1.3 collective-permute-start.5
  63.8 14.6 %window.1 = (bf16[512,1024]{1,0:T(8,128)(2,1)}, bf16[512,1024]{1,0:T(8,128)(2,1)}, bf16[512,1024]{1,0:T(8,128)(2,1)}, bf16[2,256,1024]{2,1,0:T(8,128)(2,1)}, bf16[2,256,1024]{2,1,0:T(8,128)(2,1)}) custom-call(bf16[512,1024]{1,0:T(8,128)(2,1)} %q_ref.3, bf16[512,1024]{1,0:T(8,128)(2,1)} %k_ref.3, bf16[512,1024]{1,0:T(8,128)(2,1)} %v_ref.3, ...), custom_call_target="tpu_custom_call" | custom-call | flops 2684354560 | bytes 31457280 | tf_op jit(solution)/shard_map/window/pallas_call | solution.py:79
  78.4 2.3 %collective-permute-done.6.refs_0_ = bf16[512,1024]{1,0:T(8,128)(2,1)} collective-permute-done((bf16[512,1024]{1,0:T(8,128)(2,1)}, bf16[512,1024]{1,0:T(8,128)(2,1)}, u32[]{:S(2)}, u32[]{:S(2)}) %collective-permute-start.6) | collective-permute-done | bytes 1048608 | tf_op jit(solution)/shard_map/ppermute | solution.py:267
  80.7 11.7 %collective-permute-done.5.refs_6_ = bf16[512,1024]{1,0:T(8,128)(2,1)} collective-permute-done((bf16[512,1024]{1,0:T(8,128)(2,1)S(1)}, bf16[512,1024]{1,0:T(8,128)(2,1)}, u32[]{:S(2)}, u32[]{:S(2)}) %collective-permute-start.5) | collective-permute-done | bytes 1048608 | tf_op jit(solution)/shard_map/ppermute | solution.py:255
  92.4 0.7 collective-permute-start.9
  93.1 1.3 collective-permute-start.10
  94.4 1.3 collective-permute-start.7
  95.8 4.7 %collective-permute-start.8 = (bf16[2,256,1024]{2,1,0:T(8,128)(2,1)}, bf16[2,256,1024]{2,1,0:T(8,128)(2,1)S(1)}, u32[]{:S(2)}, u32[]{:S(2)}) collective-permute-start(bf16[2,256,1024]{2,1,0:T(8,128)(2,1)} %get-tuple-element.51), channel_id=1, source_target_pairs={{0,4},{4,8},{8,12},{12,16},{16,20},{20,24},{24,28},{1,5},{5,9},{9,... | collective-permute-start | bytes 3145736 | tf_op jit(solution)/shard_map/ppermute | solution.py:260
  100.5 20.8 %collective-permute-done.10.refs_7_ = bf16[512,1024]{1,0:T(8,128)(2,1)S(1)} collective-permute-done((bf16[512,1024]{1,0:T(8,128)(2,1)}, bf16[512,1024]{1,0:T(8,128)(2,1)S(1)}, u32[]{:S(2)}, u32[]{:S(2)}) %collective-permute-start.10) | collective-permute-done | bytes 1048608 | tf_op jit(solution)/shard_map/ppermute | solution.py:255
  121.3 5.7 %parts.2 = (bf16[2,512,512]{2,1,0:T(8,128)(2,1)}, bf16[2,512,512]{2,1,0:T(8,128)(2,1)S(1)}) custom-call(bf16[512,1024]{1,0:T(8,128)(2,1)} %collective-permute-done.6.refs_0_, bf16[512,1024]{1,0:T(8,128)(2,1)S(1)} %collective-permute-done.9.refs_1_, bf16[512,1024]{1,0:T(8,128)(2,1)} %collective-permute-done.4.refs_2_, ...), custom_call_target="tpu_custom_call" | custom-call | flops 268435456 | bytes 1048576 | tf_op jit(solution)/shard_map/parts/pallas_call | solution.py:221
  127.0 0.1 collective-permute-start.11
  127.1 1.0 copy-done.8
  128.1 12.5 %collective-permute-done.8.high_ref = bf16[2,256,1024]{2,1,0:T(8,128)(2,1)S(1)} collective-permute-done((bf16[2,256,1024]{2,1,0:T(8,128)(2,1)}, bf16[2,256,1024]{2,1,0:T(8,128)(2,1)S(1)}, u32[]{:S(2)}, u32[]{:S(2)}) %collective-permute-start.8) | collective-permute-done | bytes 1048608 | tf_op jit(solution)/shard_map/ppermute | solution.py:260
  140.6 4.4 %parts.3 = (bf16[2,512,512]{2,1,0:T(8,128)(2,1)}, bf16[2,512,512]{2,1,0:T(8,128)(2,1)S(1)}) custom-call(bf16[512,1024]{1,0:T(8,128)(2,1)S(1)} %copy-done.5, bf16[512,1024]{1,0:T(8,128)(2,1)S(1)} %collective-permute-done.9.refs_1_, bf16[512,1024]{1,0:T(8,128)(2,1)} %collective-permute-done.4.refs_2_, bf16[512,1024]{1,0:T(8,128)(2,1)S(1)} %collective-permute-done.refs_3_, ...), custom_call_target="tpu_custom_call" | custom-call | flops 268435456 | bytes 1048576 | tf_op jit(solution)/shard_map/parts/pallas_call | solution.py:221
  145.1 1.0 copy-done.3
  146.0 1.1 copy.23
  147.1 4.6 %all-to-all-start = ((bf16[2,8,32,1024]{3,2,0,1:T(8,128)(2,1)}), bf16[2,8,32,1024]{3,2,0,1:T(8,128)(2,1)S(1)}, u32[]{:S(2)}, u32[]{:S(2)}) async-start(bf16[2,8,32,1024]{3,2,0,1:T(8,128)(2,1)} %copy.23), calls=%async_computation | async-start | bytes 2097152 | tf_op jit(solution)/shard_map/all_to_all | solution.py:340
  151.7 1.6 convert_add_fusion.1
  153.3 0.1 fusion.4
  153.4 0.7 collective-permute-start.12
  154.2 1.0 copy-done.10
  155.1 1.5 convert_add_fusion
  156.7 0.9 fusion.5
  157.5 1.3 collective-permute-start.15
  158.9 9.4 %collective-permute-done.12 = bf16[512,512]{1,0:T(8,128)(2,1)S(1)} collective-permute-done((bf16[512,512]{1,0:T(8,128)(2,1)S(1)}, bf16[512,512]{1,0:T(8,128)(2,1)S(1)}, u32[]{:S(2)}, u32[]{:S(2)}) %collective-permute-start.12) | collective-permute-done | bytes 524320 | tf_op jit(solution)/shard_map/ppermute | solution.py:276
  168.2 1.0 fusion.3
  169.2 2.1 %collective-permute-start.13 = (bf16[512,512]{1,0:T(8,128)(2,1)}, bf16[512,512]{1,0:T(8,128)(2,1)}, u32[]{:S(2)}, u32[]{:S(2)}) collective-permute-start(bf16[512,512]{1,0:T(8,128)(2,1)} %fusion.3), channel_id=1, source_target_pairs={{0,4},{4,0},{8,12},{12,8},{16,20},{20,16},{24,28},{28,24},{1,5},{5... | collective-permute-start | bytes 1572872 | tf_op jit(solution)/shard_map/ppermute | solution.py:267
  171.3 4.2 %join.1 = (bf16[512,1024]{1,0:T(8,128)(2,1)}, bf16[512,1024]{1,0:T(8,128)(2,1)}) custom-call(bf16[512,1024]{1,0:T(8,128)(2,1)} %get-tuple-element.47.dk_ref, bf16[512,1024]{1,0:T(8,128)(2,1)} %get-tuple-element.48.dv_ref, bf16[2,256,1024]{2,1,0:T(8,128)(2,1)} %copy-done.8, bf16[2,256,1024]{2,1,0:T(8,128)(2,1)} %copy-done.9), custom_call_target="tpu_custom_call" | custom-call | flops 1048576 | bytes 6291456 | tf_op jit(solution)/shard_map/join/pallas_call | solution.py:109
  175.4 2.7 %all-to-all-done = bf16[2,8,32,1024]{3,2,0,1:T(8,128)(2,1)S(1)} async-done(((bf16[2,8,32,1024]{3,2,0,1:T(8,128)(2,1)}), bf16[2,8,32,1024]{3,2,0,1:T(8,128)(2,1)S(1)}, u32[]{:S(2)}, u32[]{:S(2)}) %all-to-all-start) | async-done | bytes 1048608 | tf_op jit(solution)/shard_map/all_to_all | solution.py:340
  178.2 1.1 copy.24
  179.2 3.7 %collective-permute-done.13 = bf16[512,512]{1,0:T(8,128)(2,1)} collective-permute-done((bf16[512,512]{1,0:T(8,128)(2,1)}, bf16[512,512]{1,0:T(8,128)(2,1)}, u32[]{:S(2)}, u32[]{:S(2)}) %collective-permute-start.13) | collective-permute-done | bytes 524320 | tf_op jit(solution)/shard_map/ppermute | solution.py:267
  183.0 1.4 broadcast_select_fusion.1
  184.4 1.1 pad_maximum_fusion.2
  (33 shorter events, 0.1 us)
Async XLA Ops:
  0.6 7.7 %copy-start.6 = (bf16[512,1024]{1,0:T(8,128)(2,1)S(1)}, bf16[512,1024]{1,0:T(8,128)(2,1)}, u32[]{:S(2)}) copy-start(bf16[512,1024]{1,0:T(8,128)(2,1)} %k_ref.3) | copy-start | bytes 3145732
  0.6 28.1 %collective-permute-start = (bf16[512,1024]{1,0:T(8,128)(2,1)}, bf16[512,1024]{1,0:T(8,128)(2,1)S(1)}, u32[]{:S(2)}, u32[]{:S(2)}) collective-permute-start(bf16[512,1024]{1,0:T(8,128)(2,1)} %refs_4_.3), channel_id=1, source_target_pairs={{0,8},{4,12},{8,16},{12,20},{16,24},{20,28},{1,9},{5,13},{9,17},{1... | collective-permute-start | bytes 3145736 | tf_op jit(solution)/shard_map/ppermute | solution.py:255
  5.8 28.2 %collective-permute-start.1 = (bf16[512,1024]{1,0:T(8,128)(2,1)}, bf16[512,1024]{1,0:T(8,128)(2,1)S(1)}, u32[]{:S(2)}, u32[]{:S(2)}) collective-permute-start(bf16[512,1024]{1,0:T(8,128)(2,1)} %refs_4_.3), channel_id=1, source_target_pairs={{28,20},{24,16},{20,12},{16,8},{12,4},{8,0},{29,21},{25,17},{21,13... | collective-permute-start | bytes 3145736 | tf_op jit(solution)/shard_map/ppermute | solution.py:255
  8.4 6.3 %copy-start.11 = (s32[2,64]{1,0:T(2,128)S(1)}, s32[2,64]{1,0:T(2,128)}, u32[]{:S(2)}) copy-start(s32[2,64]{1,0:T(2,128)} %param.19) | copy-start | bytes 1540
  8.5 7.1 %copy-start.12 = (s32[128,1]{0,1:T(1,128)S(1)}, s32[128,1]{0,1:T(1,128)}, u32[]{:S(2)}) copy-start(s32[128,1]{0,1:T(1,128)} %param.20) | copy-start | bytes 1540
  10.0 49.8 %collective-permute-start.2 = (bf16[2,256,1024]{2,1,0:T(8,128)(2,1)}, bf16[2,256,1024]{2,1,0:T(8,128)(2,1)S(1)}, u32[]{:S(2)}, u32[]{:S(2)}) collective-permute-start(bf16[2,256,1024]{2,1,0:T(8,128)(2,1)} %get-tuple-element.38), channel_id=1, source_target_pairs={{0,4},{4,8},{8,12},{12,16},{16,20},{20,24},{24,28},{1,5},{5,9},{9,... | collective-permute-start | bytes 3145736 | tf_op jit(solution)/shard_map/ppermute | solution.py:260
  13.4 46.3 %collective-permute-start.3 = (bf16[2,256,1024]{2,1,0:T(8,128)(2,1)}, bf16[2,256,1024]{2,1,0:T(8,128)(2,1)}, u32[]{:S(2)}, u32[]{:S(2)}) collective-permute-start(bf16[2,256,1024]{2,1,0:T(8,128)(2,1)} %get-tuple-element.39), channel_id=1, source_target_pairs={{4,0},{8,4},{12,8},{16,12},{20,16},{24,20},{28,24},{5,1},{9,5},{13... | collective-permute-start | bytes 3145736 | tf_op jit(solution)/shard_map/ppermute | solution.py:260
  25.6 55.1 %collective-permute-start.6 = (bf16[512,1024]{1,0:T(8,128)(2,1)}, bf16[512,1024]{1,0:T(8,128)(2,1)}, u32[]{:S(2)}, u32[]{:S(2)}) collective-permute-start(bf16[512,1024]{1,0:T(8,128)(2,1)} %get-tuple-element.64.refs_0_), channel_id=1, source_target_pairs={{0,4},{4,0},{8,12},{12,8},{16,20},{20,16},{24,28},{28,24},{1,5},{5... | collective-permute-start | bytes 3145736 | tf_op jit(solution)/shard_map/ppermute | solution.py:267
  59.7 1.0 copy-start.13
  60.7 60.6 %copy-start = (bf16[512,1024]{1,0:T(8,128)(2,1)S(1)}, bf16[512,1024]{1,0:T(8,128)(2,1)}, u32[]{:S(2)}) copy-start(bf16[512,1024]{1,0:T(8,128)(2,1)} %refs_4_.3) | copy-start | bytes 3145732
  60.7 20.0 %collective-permute-start.4 = (bf16[512,1024]{1,0:T(8,128)(2,1)S(1)}, bf16[512,1024]{1,0:T(8,128)(2,1)}, u32[]{:S(2)}, u32[]{:S(2)}) collective-permute-start(bf16[512,1024]{1,0:T(8,128)(2,1)S(1)} %collective-permute-done.refs_3_), channel_id=1, source_target_pairs={{8,16},{12,20},{16,24},{20,28},{9,17},{13,21},{17,25},{21,29},{10,... | collective-permute-start | bytes 3145736 | tf_op jit(solution)/shard_map/ppermute | solution.py:255
  62.5 29.9 %collective-permute-start.5 = (bf16[512,1024]{1,0:T(8,128)(2,1)S(1)}, bf16[512,1024]{1,0:T(8,128)(2,1)}, u32[]{:S(2)}, u32[]{:S(2)}) collective-permute-start(bf16[512,1024]{1,0:T(8,128)(2,1)S(1)} %collective-permute-done.1.refs_5_), channel_id=1, source_target_pairs={{20,12},{16,8},{12,4},{8,0},{21,13},{17,9},{13,5},{9,1},{22,14},{1... | collective-permute-start | bytes 3145736 | tf_op jit(solution)/shard_map/ppermute | solution.py:255
  92.4 8.1 %collective-permute-start.9 = (bf16[512,1024]{1,0:T(8,128)(2,1)}, bf16[512,1024]{1,0:T(8,128)(2,1)S(1)}, u32[]{:S(2)}, u32[]{:S(2)}) collective-permute-start(bf16[512,1024]{1,0:T(8,128)(2,1)} %collective-permute-done.4.refs_2_), channel_id=1, source_target_pairs={{16,24},{20,28},{17,25},{21,29},{18,26},{22,30},{19,27},{23,31}} | collective-permute-start | bytes 3145736 | tf_op jit(solution)/shard_map/ppermute | solution.py:255
  93.1 28.2 %collective-permute-start.10 = (bf16[512,1024]{1,0:T(8,128)(2,1)}, bf16[512,1024]{1,0:T(8,128)(2,1)S(1)}, u32[]{:S(2)}, u32[]{:S(2)}) collective-permute-start(bf16[512,1024]{1,0:T(8,128)(2,1)} %collective-permute-done.5.refs_6_), channel_id=1, source_target_pairs={{12,4},{8,0},{13,5},{9,1},{14,6},{10,2},{15,7},{11,3}} | collective-permute-start | bytes 3145736 | tf_op jit(solution)/shard_map/ppermute | solution.py:255
  94.4 32.7 %collective-permute-start.7 = (bf16[2,256,1024]{2,1,0:T(8,128)(2,1)}, bf16[2,256,1024]{2,1,0:T(8,128)(2,1)S(1)}, u32[]{:S(2)}, u32[]{:S(2)}) collective-permute-start(bf16[2,256,1024]{2,1,0:T(8,128)(2,1)} %get-tuple-element.50), channel_id=1, source_target_pairs={{4,0},{8,4},{12,8},{16,12},{20,16},{24,20},{28,24},{5,1},{9,5},{13... | collective-permute-start | bytes 3145736 | tf_op jit(solution)/shard_map/ppermute | solution.py:260
  95.7 44.9 %copy-start.5 = (bf16[512,1024]{1,0:T(8,128)(2,1)S(1)}, bf16[512,1024]{1,0:T(8,128)(2,1)}, u32[]{:S(2)}) copy-start(bf16[512,1024]{1,0:T(8,128)(2,1)} %get-tuple-element.64.refs_0_) | copy-start | bytes 3145732
  95.8 44.9 %collective-permute-start.8 = (bf16[2,256,1024]{2,1,0:T(8,128)(2,1)}, bf16[2,256,1024]{2,1,0:T(8,128)(2,1)S(1)}, u32[]{:S(2)}, u32[]{:S(2)}) collective-permute-start(bf16[2,256,1024]{2,1,0:T(8,128)(2,1)} %get-tuple-element.51), channel_id=1, source_target_pairs={{0,4},{4,8},{8,12},{12,16},{16,20},{20,24},{24,28},{1,5},{5,9},{9,... | collective-permute-start | bytes 3145736 | tf_op jit(solution)/shard_map/ppermute | solution.py:260
  127.0 18.0 %copy-start.1 = (bf16[2,512,512]{2,1,0:T(8,128)(2,1)}, bf16[2,512,512]{2,1,0:T(8,128)(2,1)S(1)}, u32[]{:S(2)}) copy-start(bf16[2,512,512]{2,1,0:T(8,128)(2,1)S(1)} %get-tuple-element.63) | copy-start | bytes 3145732
  127.0 19.0 %copy-start.7 = (bf16[2,256,1024]{2,1,0:T(8,128)(2,1)S(1)}, bf16[2,256,1024]{2,1,0:T(8,128)(2,1)}, u32[]{:S(2)}) copy-start(bf16[2,256,1024]{2,1,0:T(8,128)(2,1)} %get-tuple-element.61) | copy-start | bytes 3145732
  127.0 24.7 %collective-permute-start.11 = (bf16[2,512,512]{2,1,0:T(8,128)(2,1)}, bf16[2,512,512]{2,1,0:T(8,128)(2,1)}, u32[]{:S(2)}, u32[]{:S(2)}) collective-permute-start(bf16[2,512,512]{2,1,0:T(8,128)(2,1)} %get-tuple-element.62), channel_id=1, source_target_pairs={{0,1},{1,0},{2,3},{3,2},{4,5},{5,4},{6,7},{7,6},{8,9},{9,8},{10,11... | collective-permute-start | bytes 3145736 | tf_op jit(solution)/shard_map/ppermute | solution.py:274
  127.1 1.0 copy-start.8
  140.6 4.4 %copy-start.9 = (bf16[2,256,1024]{2,1,0:T(8,128)(2,1)}, bf16[2,256,1024]{2,1,0:T(8,128)(2,1)S(1)}, u32[]{:S(2)}) copy-start(bf16[2,256,1024]{2,1,0:T(8,128)(2,1)S(1)} %collective-permute-done.8.high_ref) | copy-start | bytes 3145732
  145.1 1.0 copy-start.3
  146.0 8.1 %collective-permute-start.14 = (bf16[2,512,512]{2,1,0:T(8,128)(2,1)}, bf16[2,512,512]{2,1,0:T(8,128)(2,1)S(1)}, u32[]{:S(2)}, u32[]{:S(2)}) collective-permute-start(bf16[2,512,512]{2,1,0:T(8,128)(2,1)} %get-tuple-element.65), channel_id=1, source_target_pairs={{0,1},{1,0},{2,3},{3,2},{4,5},{5,4},{6,7},{7,6},{8,9},{9,8},{10,11... | collective-permute-start | bytes 3145736 | tf_op jit(solution)/shard_map/ppermute | solution.py:274
  146.0 5.7 %copy-start.2 = (bf16[2,512,512]{2,1,0:T(8,128)(2,1)S(1)}, bf16[2,512,512]{2,1,0:T(8,128)(2,1)}, u32[]{:S(2)}) copy-start(bf16[2,512,512]{2,1,0:T(8,128)(2,1)} %copy-done.1) | copy-start | bytes 3145732
  147.1 31.1 %all-to-all-start = ((bf16[2,8,32,1024]{3,2,0,1:T(8,128)(2,1)}), bf16[2,8,32,1024]{3,2,0,1:T(8,128)(2,1)S(1)}, u32[]{:S(2)}, u32[]{:S(2)}) async-start(bf16[2,8,32,1024]{3,2,0,1:T(8,128)(2,1)} %copy.23), calls=%async_computation | async-start | bytes 2097152 | tf_op jit(solution)/shard_map/all_to_all | solution.py:340
  151.7 3.4 %copy-start.4 = (bf16[2,512,512]{2,1,0:T(8,128)(2,1)S(1)}, bf16[2,512,512]{2,1,0:T(8,128)(2,1)}, u32[]{:S(2)}) copy-start(bf16[2,512,512]{2,1,0:T(8,128)(2,1)} %copy-done.3) | copy-start | bytes 3145732
  153.4 14.8 %collective-permute-start.12 = (bf16[512,512]{1,0:T(8,128)(2,1)S(1)}, bf16[512,512]{1,0:T(8,128)(2,1)S(1)}, u32[]{:S(2)}, u32[]{:S(2)}) collective-permute-start(bf16[512,512]{1,0:T(8,128)(2,1)S(1)} %fusion.4), channel_id=1, source_target_pairs={{0,2},{1,3},{2,0},{3,1},{4,6},{5,7},{6,4},{7,5},{8,10},{9,11},{10,... | collective-permute-start | bytes 1572872 | tf_op jit(solution)/shard_map/ppermute | solution.py:276
  154.1 1.0 copy-start.10
  157.5 21.7 %collective-permute-start.15 = (bf16[512,512]{1,0:T(8,128)(2,1)}, bf16[512,512]{1,0:T(8,128)(2,1)}, u32[]{:S(2)}, u32[]{:S(2)}) collective-permute-start(bf16[512,512]{1,0:T(8,128)(2,1)} %fusion.5), channel_id=1, source_target_pairs={{0,2},{1,3},{2,0},{3,1},{4,6},{5,7},{6,4},{7,5},{8,10},{9,11},{10,... | collective-permute-start | bytes 1572872 | tf_op jit(solution)/shard_map/ppermute | solution.py:276
  169.2 13.8 %collective-permute-start.13 = (bf16[512,512]{1,0:T(8,128)(2,1)}, bf16[512,512]{1,0:T(8,128)(2,1)}, u32[]{:S(2)}, u32[]{:S(2)}) collective-permute-start(bf16[512,512]{1,0:T(8,128)(2,1)} %fusion.3), channel_id=1, source_target_pairs={{0,4},{4,0},{8,12},{12,8},{16,20},{20,16},{24,28},{28,24},{1,5},{5... | collective-permute-start | bytes 1572872 | tf_op jit(solution)/shard_map/ppermute | solution.py:267
